TPU v7x, 256 devices: a whole 4x4x8 slice. The times are simulated.
256 devices in a mesh: rep: 32 (over y, x, core), fsdp: 8 (over z).
Axes of the slice: x: 4, y: 4, z: 8, core: 2. Of those that a mesh axis runs over, the one named last changes fastest.
Arguments:
- codes: bfloat16 [32, 4096, 1024], P('rep', 'fsdp'), may hold values from -127 to 127
- block_scales: float32 [32, 4096, 8], P('rep', 'fsdp'), may hold values from 0.002 to 0.02
- params: bfloat16 [4096, 1024], P('fsdp'), may hold values from -6 to 6
- momentum: bfloat16 [4096, 1024], P('fsdp'), may hold values from -3 to 3
Outputs:
- new_params: bfloat16 [4096, 1024], replicated
- new_momentum: bfloat16 [4096, 1024], P('fsdp')
All inputs are finite; a program needn't handle non-finite values.
Results may differ from a plain program's by a relative error of at most 0.006.
Values may be sent and summed in bfloat16 or wider, within the bound.
A program may use at most 64 MiB of HBM per device.

v0:
```python
import jax
import jax.numpy as jnp
from jax import lax
from jax.sharding import Mesh
from jax.sharding import PartitionSpec as P

REP = ("rep_0", "rep_1", "rep_2")


def filled_up(lines, peers):
    spare = -len(lines) % peers
    return jnp.pad(lines, [(0, spare)] + [(0, 0)] * (lines.ndim - 1))


def sent_to_all(shard, axis):
    copies = jnp.broadcast_to(shard, (lax.axis_size(axis), *shard.shape))
    return lax.all_to_all(copies, axis, split_axis=0, concat_axis=0, tiled=True)


def joined_along(blocks, dim):
    blocks = jnp.moveaxis(blocks, 0, dim)
    lengths = blocks.shape
    return blocks.reshape(*lengths[:dim], lengths[dim] * lengths[dim + 1], *lengths[dim + 2 :])


def whole_of(shard, axes, dim):
    far, near = axes
    first = sent_to_all(shard, far)
    blocks = jnp.swapaxes(sent_to_all(first, near), 0, 1)
    return joined_along(blocks.reshape(-1, *shard.shape), dim)


def in_blocks(shard, dim, peers):
    before, after = (shard.shape[:dim], shard.shape[dim + 1 :])
    return jnp.moveaxis(shard.reshape(*before, peers, -1, *after), dim, 0)


def sum_at_owner(shard, axis, dim):
    blocks = in_blocks(shard, dim, lax.axis_size(axis))
    arrived = lax.all_to_all(blocks, axis, split_axis=0, concat_axis=0, tiled=True)
    return arrived.astype(jnp.float32).sum(axis=0)


def summed_rows(shard, axes, dim):
    far, near = axes
    own = sum_at_owner(in_blocks(shard, dim, lax.axis_size(far)), near, dim + 1)
    return jnp.sum(
        lax.all_to_all(own.astype(jnp.bfloat16), far, 0, 0, tiled=True).astype(jnp.float32), axis=0
    )


def sum_by_parts(shard, axes):
    lines = shard.reshape(-1, shard.shape[-1])
    padded = filled_up(lines, lax.axis_size(axes[0]) * lax.axis_size(axes[1]))
    whole = whole_of(summed_rows(padded, axes, 0).astype(jnp.bfloat16), axes, 0)
    return lax.slice_in_dim(whole, 0, len(lines)).reshape(shard.shape).astype(jnp.float32)


def dequantize(code_rows, scale_rows):
    count, width = code_rows.shape
    pieces = (
        code_rows.astype(jnp.float32).reshape(count, width // 128, 128) * scale_rows[:, :, None]
    )
    return pieces.reshape(count, width)


def outer_update(total, params, momentum, replicas):
    delta = total / replicas
    moment = 0.9 * momentum.astype(jnp.float32) + delta
    updated = (params.astype(jnp.float32) - 0.7 * (delta + 0.9 * moment)).astype(jnp.bfloat16)
    return (updated, moment.astype(jnp.bfloat16))


def local(codes, block_scales, params, momentum):
    replicas = lax.axis_size(REP)
    local_term = dequantize(codes[0], block_scales[0])
    total = sum_by_parts(local_term.astype(jnp.bfloat16), (("rep_0", "rep_1"), "rep_2"))
    updated, new_momentum = outer_update(total, params, momentum, replicas)
    new_params = lax.all_gather(updated, "fsdp", axis=0, tiled=True)
    return (new_params, new_momentum)


def solution(mesh):
    finer = Mesh(
        mesh.devices.reshape(4, 4, 2, mesh.shape["fsdp"]), ("rep_0", "rep_1", "rep_2", "fsdp")
    )
    placed = (P(REP, "fsdp", None), P(REP, "fsdp", None), P("fsdp", None), P("fsdp", None))
    return jax.shard_map(
        local, mesh=finer, in_specs=placed, out_specs=(P(), P("fsdp", None)), check_vma=False
    )
```

profile of v0, /device:TPU:1, one launch (start us, length us, event | category | flops | bytes accessed | tf_op | source)
XLA Modules:
  0.0 167.0 jit_solution(15279222004547587232)
XLA Ops:
  7.2 0.0 all-gather.2.cloned.1.call-start
  7.2 0.8 copy.11
  8.1 0.6 mul.27
  8.7 0.0 copy-start
  8.7 1.5 mul.28
  10.2 0.0 copy-done
  10.2 1.9 %fusion.5 = bf16[2,16,16,1024]{3,2,0,1:T(8,128)(2,1)S(1)} fusion(f32[16,2,16,1024]{3,2,1,0:T(8,128)} %mul.28, bf16[16,2,16,1024]{3,2,1,0:T(8,128)(2,1)S(1)} %bitcast.20), kind=kLoop, calls=%fused_computation.9 | loop fusion | flops 1572864 | bytes 4194304 | tf_op jit(solution)/shard_map/transpose | solution.py:35
  12.1 0.1 copy.12
  12.2 7.4 %all_to_all.20 = bf16[2,16,16,1024]{3,2,1,0:T(8,128)(2,1)S(1)} all-to-all(bf16[2,16,16,1024]{3,2,1,0:T(8,128)(2,1)S(1)} %copy.12), channel_id=1, replica_groups=mesh['rep_0'=4,'rep_1'=4,'rep_2'=2,'fsdp'=8] {'rep_2'}, dimensions={0} | all-to-all | bytes 2097152 | tf_op jit(solution)/shard_map/all_to_all | solution.py:40
  19.6 0.3 reduce_sum.24
  19.9 15.5 %all_to_all.21 = bf16[16,16,1024]{2,1,0:T(8,128)(2,1)S(1)} all-to-all(bf16[16,16,1024]{2,1,0:T(8,128)(2,1)S(1)} %reduce_sum.24), channel_id=1, replica_groups=mesh['rep_0'=4,'rep_1'=4,'rep_2'=2,'fsdp'=8] {'rep_0','rep_1'}, dimensions={0} | all-to-all | bytes 1048576 | tf_op jit(solution)/shard_map/all_to_all | solution.py:48
  35.4 0.1 reduce_sum.25
  35.5 0.1 broadcast_in_dim.6
  35.6 13.4 %all_to_all.22 = bf16[16,16,1024]{2,1,0:T(8,128)(2,1)S(1)} all-to-all(bf16[16,16,1024]{2,1,0:T(8,128)(2,1)S(1)} %broadcast_in_dim.6), channel_id=1, replica_groups=mesh['rep_0'=4,'rep_1'=4,'rep_2'=2,'fsdp'=8] {'rep_0','rep_1'}, dimensions={0} | all-to-all | bytes 1048576 | tf_op jit(solution)/shard_map/all_to_all | solution.py:17
  49.0 0.1 broadcast_in_dim.7
  49.1 6.5 %all_to_all.23 = bf16[2,16,16,1024]{3,2,1,0:T(8,128)(2,1)S(1)} all-to-all(bf16[2,16,16,1024]{3,2,1,0:T(8,128)(2,1)S(1)} %broadcast_in_dim.7), channel_id=1, replica_groups=mesh['rep_0'=4,'rep_1'=4,'rep_2'=2,'fsdp'=8] {'rep_2'}, dimensions={0} | all-to-all | bytes 2097152 | tf_op jit(solution)/shard_map/all_to_all | solution.py:17
  55.7 0.0 copy-start.1
  55.7 0.0 copy-start.2
  55.7 0.3 convert_multiply_fusion.1
  55.9 1.0 copy-done.1
  56.9 0.3 copy-done.2
  57.2 2.0 %fusion.4 = (bf16[512,1024]{1,0:T(8,128)(2,1)}, bf16[512,1024]{1,0:T(8,128)(2,1)}) fusion(f32[2,16,16,1024]{3,2,0,1:T(8,128)S(1)} %convert_multiply_fusion.1, bf16[512,1024]{1,0:T(8,128)(2,1)S(1)} %copy-done.1, bf16[512,1024]{1,0:T(8,128)(2,1)S(1)} %copy-done.2), kind=kLoop, calls=%fused_computation.7 | loop fusion | flops 5242880 | bytes 6291456 | tf_op jit(solution)/shard_map/convert_element_type | solution.py:71
  59.3 0.0 all-gather.2.cloned.1.call-update
  59.3 93.1 %all-gather.2.cloned.1.call-done = bf16[4096,1024]{1,0:T(8,128)(2,1)} async-done(((bf16[512,1024]{1,0:T(8,128)(2,1)}), bf16[4096,1024]{1,0:T(8,128)(2,1)}) %all-gather.2.cloned.1.call-update) | async-done | bytes 8388624 | tf_op jit(solution)/shard_map/all_gather | solution.py:79
  152.4 7.8 %copy.16 = bf16[4096,1024]{1,0:T(8,128)(2,1)} copy(bf16[4096,1024]{1,0:T(8,128)(2,1)} %all-gather.2.cloned.1.call-done) | data formatting | bytes 16777216
Async XLA Ops:
  7.2 145.2 %all-gather.2.cloned.1.call-start = ((), (), s32[]{:S(2)}) async-start(), calls=%async_computation.4 | async-start | bytes 9437184 | tf_op jit(solution)/shard_map/all_gather | solution.py:79
  8.7 1.5 copy-start
  55.7 1.2 copy-start.1
  55.7 1.5 copy-start.2
Sparse Core Ops, SparseCore 0:
  59.4 92.9 all-gather.1
where the time goes:
time: 167 us
  waiting for transfers between devices  93.1 us (56%)
  blocking collectives  42.9 us (26%)
  between operations  14.1 us (8%)
  local copies, waits for them, and re-layouts  12.2 us (7%)
  other arithmetic  4.57 us (3%)
    all_gather x1, waiting for transfers between devices, local(): new_params = lax.all_gather(updated, 'fsdp', axis=0, tiled=True)  93.1 us
    all_to_all x2, blocking collectives, sent_to_all(): return lax.all_to_all(copies, axis, split_axis=0, concat_axis=0, tiled=True)  20 us
    all_to_all x1, blocking collectives, summed_rows(): lax.all_to_all(own.astype(jnp.bfloat16), far, 0, 0, tiled=True)  15.5 us
    unnamed x7, local copies, waits for them, and re-layouts  9.05 us
    all_to_all x1, blocking collectives, sum_at_owner(): lax.all_to_all(blocks, axis, split_axis=0, concat_axis=0, tiled=True)  7.44 us
  transfers between devices with their start and end apart: 1, of which 1 were waited for; matrix products, arithmetic and copies ran while one was open for 0% of the time, Pallas kernels for 0%

commit v1 on v0

v1 whole, which is shorter than its diff:
```python
import functools

import jax
import jax.numpy as jnp
from jax import lax
from jax.experimental import pallas as pl
from jax.experimental.pallas import tpu as pltpu
from jax.sharding import PartitionSpec as P

MESH = pl.DeviceIdType.MESH
NX, NY, NZ = 4, 4, 8
ROWS, COLS, BLOCK = 512, 1024, 128
HALF = ROWS // 2
PIECE = 16
NEAR = (0, 1, -1, 2, -2, 3, -3, 4)
PLACE = {d: i for i, d in enumerate(NEAR)} | {-4: 7}
A, B, C = (0, 384), (384, 384), (768, 256)
AB = 768
WAVES = ((0, 1), (1, 2), (3, 2), (5, 3))
PLANE = [(dx, dy) for dy in (0, 1, -1, 2) for dx in (0, 1, -1, 2) if (dx, dy) != (0, 0)]
COPIES = 160


def position():
    r, z = lax.axis_index("rep"), lax.axis_index("fsdp")
    return lax.rem(lax.div(r, 2), NX), lax.div(r, 2 * NX), z, lax.rem(r, 2)


def step_of(delta, params, momentum):
    delta = delta.astype(jnp.float32)
    moment = 0.9 * momentum.astype(jnp.float32) + delta
    updated = params.astype(jnp.float32) - 0.7 * (delta + 0.9 * moment)
    return updated.astype(jnp.bfloat16), moment.astype(jnp.bfloat16)


def exchange(codes, scales, params, momentum, full, own_params, own_moment,
             codes_v, scales_v, params_v, momentum_v, sib_out, sib_in, chip_sum, arrived, piece, ring,
             load_sem, send_sem, recv_sem):
    x, y, z, c = position()
    other = 1 - c

    def device(dx=0, dy=0, dz=0, dc=0):
        rep = (lax.rem(y + dy + NY, NY) * NX + lax.rem(x + dx + NX, NX)) * 2 + (other if dc else c)
        return rep, lax.rem(z + dz + NZ, NZ)

    loads = [pltpu.make_async_copy(src, dst, load_sem.at[i]) for i, (src, dst) in enumerate(
        ((codes, codes_v), (scales, scales_v), (params, params_v), (momentum, momentum_v)))]
    for load in loads:
        load.start()

    barrier = pltpu.get_barrier_semaphore()
    partners = [dict(dc=1)] + [dict(dx=dx, dy=dy) for dx, dy in PLANE] + [dict(dz=dz) for dz in NEAR[1:]]
    for partner in partners:
        pl.semaphore_signal(barrier, inc=1, device_id=device(**partner), device_id_type=MESH)

    sent = []

    def send(src, dst, **to):
        i = len(sent)
        copy = pltpu.make_async_remote_copy(src, dst, send_sem.at[i], recv_sem.at[i],
                                            device_id=device(**to), device_id_type=MESH)
        copy.start()
        sent.append(copy)
        return copy

    def got(*copies):
        for copy in copies:
            copy.wait_recv()

    def dequantized(half, chunk, block):
        start = pl.multiple_of(half * HALF + chunk * 128, 128)
        turned = scales_v[:, pl.ds(start, 128)].T
        codes_f = codes_v[pl.ds(start, 128), block * BLOCK:(block + 1) * BLOCK].astype(jnp.float32)
        return codes_f * turned[:, block:block + 1]

    loads[0].wait()
    loads[1].wait()
    halves = []
    for chunk in range(2):
        rows = slice(chunk * 128, (chunk + 1) * 128)
        for block in range(8):
            sib_out[rows, block * BLOCK:(block + 1) * BLOCK] = dequantized(other, chunk, block).astype(jnp.bfloat16)
        if chunk == 0:
            pl.semaphore_wait(barrier, len(partners))
        halves.append(send(sib_out.at[rows], sib_in.at[rows], dc=1))
    for chunk in range(2):
        rows = slice(chunk * 128, (chunk + 1) * 128)
        got(halves[chunk])
        for block in range(8):
            cols = slice(block * BLOCK, (block + 1) * BLOCK)
            total = dequantized(c, chunk, block) + sib_in[rows, cols].astype(jnp.float32)
            chip_sum[2 * chunk:2 * chunk + 2, :, :, cols] = total.astype(jnp.bfloat16).reshape(2, NX, PIECE, BLOCK)

    pieces = []
    for i, (dx, dy) in enumerate(PLANE):
        theirs = chip_sum.at[lax.rem(y + dy + NY, NY), lax.rem(x + dx + NX, NX)]
        pieces.append(send(theirs, arrived.at[i], dx=dx, dy=dy))
    loads[2].wait()
    loads[3].wait()
    total = chip_sum[y, x].astype(jnp.float32)
    for i, copy in enumerate(pieces):
        got(copy)
        total = total + arrived[i].astype(jnp.float32)
    delta = (total / 32).astype(jnp.bfloat16)
    start = pl.multiple_of(c * HALF + y * 64 + x * PIECE, PIECE)
    full[0, c, y, x] = delta
    piece[...] = step_of(delta, params_v[pl.ds(start, PIECE)], momentum_v[pl.ds(start, PIECE)])[0]

    def at(place, count, rows_y, rows_x, group):
        return full.at[pl.ds(place, count), c, rows_y, rows_x, :, pl.ds(*group)]

    def second(wave, group):
        block = at(*WAVES[wave], y, x, group)
        return [send(block, block, **{"dx" if group is A else "dy": d}) for d in (1, -1, 2)]

    def halves_of(wave, group, back):
        for i in range(2):
            if group is A:
                yield at(*WAVES[wave], lax.rem(y - back + NY, NY), pl.ds(2 * i, 2), group)
            else:
                yield at(*WAVES[wave], pl.ds(2 * i, 2), lax.rem(x - back + NX, NX), group)

    def third(wave, group):
        axis = "dy" if group is A else "dx"
        one, two = halves_of(wave, group, 0)
        return (send(one, one, **{axis: 1}), send(two, two, **{axis: -1}),
                send(two, two, **{axis: 1}), send(one, one, **{axis: -1}))

    def onward(wave, group, copies):
        axis = "dy" if group is A else "dx"
        one, _ = halves_of(wave, group, 1)
        _, two = halves_of(wave, group, -1)
        got(copies[0])
        ahead = send(one, one, **{axis: 1})
        got(copies[1])
        return (*copies[2:], ahead, send(two, two, **{axis: -1}))

    def to_sibling(place, count, group):
        block = full.at[pl.ds(place, count), c, :, :, :, pl.ds(*group)]
        return send(block, block, dc=1)

    S2, S3, S4, handed = {}, {}, {}, []

    for group in (A, B):
        S2[0, group] = second(0, group)
    plane_c = []
    block = full.at[0, c, y, x, :, pl.ds(*C)]
    for dx, dy in PLANE:
        plane_c.append(send(block, block, dx=dx, dy=dy))
    along = {}
    for dz in NEAR[1:]:
        place = PLACE[-dz]
        along[place] = send(piece.at[:, pl.ds(0, AB)], full.at[place, c, y, x, :, pl.ds(0, AB)], dz=dz)

    def start_second(wave):
        first, count = WAVES[wave]
        got(*(along[i] for i in range(first, first + count)))
        for group in (A, B):
            S2[wave, group] = second(wave, group)

    def start_third(wave):
        for group in (A, B):
            got(*S2[wave, group])
            S3[wave, group] = third(wave, group)

    def start_onward(wave):
        for group in (A, B):
            S4[wave, group] = onward(wave, group, S3[wave, group])

    def finish(wave):
        for group in (A, B):
            got(*S4[wave, group])
            handed.append(to_sibling(*WAVES[wave], group))

    def ring_at(d, rows=slice(None)):
        return full.at[PLACE[d], c, rows, :, :, pl.ds(*C)]

    up, down = {}, {}

    def ring_step(n):
        got(up[n])
        got(down[n])
        if n < 3:
            up[n + 1] = send(ring_at(-n), ring_at(-n - 1), dz=1)
            down[n + 1] = send(ring_at(n), ring_at(n + 1), dz=-1)
        elif n == 3:
            up[4] = send(ring_at(-3, pl.ds(0, 2)), ring_at(4, pl.ds(0, 2)), dz=1)
            down[4] = send(ring_at(3, pl.ds(2, 2)), ring_at(4, pl.ds(2, 2)), dz=-1)
        if n < 4:
            handed.append(to_sibling(PLACE[n], 2, C))
        else:
            handed.append(to_sibling(PLACE[4], 1, C))

    start_third(0)
    start_second(1)
    got(*plane_c)
    for row in range(NY):
        start = pl.multiple_of(c * HALF + row * 64, 64)
        moved = full[0, c, row, :, :, C[0]:C[0] + C[1]].reshape(64, C[1])
        cols = slice(C[0], C[0] + C[1])
        ring[row] = step_of(moved, params_v[pl.ds(start, 64), cols], momentum_v[pl.ds(start, 64), cols])[0].reshape(
            NX, PIECE, C[1])
    up[1] = send(ring, ring_at(-1), dz=1)
    down[1] = send(ring, ring_at(1), dz=-1)
    handed.append(to_sibling(0, 1, C))
    start_second(2)
    start_onward(0)
    start_third(1)
    start_second(3)
    finish(0)
    ring_step(1)
    start_third(2)
    start_onward(1)
    start_third(3)
    ring_step(2)
    finish(1)

    got(*handed[:3])
    del handed[:3]
    for i in range(2):
        for row in range(NY):
            start = i * HALF + row * 64
            moved = full[0, i, row].reshape(64, COLS)
            updated, moment = step_of(moved, params_v[start:start + 64], momentum_v[start:start + 64])
            own_params[start:start + 64] = updated
            own_moment[start:start + 64] = moment

    start_onward(2)
    ring_step(3)
    finish(2)
    start_onward(3)
    finish(3)
    ring_step(4)
    got(*handed)
    for copy in sent:
        copy.wait_send()


def write_out(full, own_params, own_moment, new_params, new_momentum, sem):
    z = lax.axis_index("fsdp")
    copies = []
    for i, d in enumerate(NEAR[1:], 1):
        copies.append(pltpu.make_async_copy(full.at[i], new_params.at[lax.rem(z + d + NZ, NZ)], sem.at[i]))
    copies.append(pltpu.make_async_copy(own_params, new_params.at[z], sem.at[0]))
    copies.append(pltpu.make_async_copy(own_moment, new_momentum, sem.at[8]))
    for copy in copies:
        copy.start()
    for copy in copies:
        copy.wait()


def local(codes, block_scales, params, momentum):
    bf16 = jnp.bfloat16
    slab = (2, NY, NX, PIECE, COLS)
    hbm, vmem = pl.BlockSpec(memory_space=pltpu.HBM), pl.BlockSpec(memory_space=pltpu.VMEM)
    full, own_params, own_moment = pl.pallas_call(
        exchange,
        name="exchange",
        out_shape=(pltpu.VMEM((NZ, *slab), bf16), pltpu.VMEM((ROWS, COLS), bf16), pltpu.VMEM((ROWS, COLS), bf16)),
        in_specs=[hbm] * 4,
        out_specs=[vmem] * 3,
        scratch_shapes=[
            pltpu.VMEM((ROWS, COLS), bf16),
            pltpu.VMEM((COLS // BLOCK, ROWS), jnp.float32),
            pltpu.VMEM((ROWS, COLS), bf16),
            pltpu.VMEM((ROWS, COLS), bf16),
            pltpu.VMEM((HALF, COLS), bf16),
            pltpu.VMEM((HALF, COLS), bf16),
            pltpu.VMEM((NY, NX, PIECE, COLS), bf16),
            pltpu.VMEM((len(PLANE), PIECE, COLS), bf16),
            pltpu.VMEM((PIECE, COLS), bf16),
            pltpu.VMEM((NY, NX, PIECE, C[1]), bf16),
            pltpu.SemaphoreType.DMA((4,)),
            pltpu.SemaphoreType.DMA((COPIES,)),
            pltpu.SemaphoreType.DMA((COPIES,)),
        ],
        compiler_params=pltpu.CompilerParams(
            collective_id=0, has_side_effects=True, vmem_limit_bytes=32 * 2**20
        ),
    )(codes[0], block_scales[0].T, params, momentum)
    new_params, new_momentum = pl.pallas_call(
        write_out,
        name="write_out",
        out_shape=(jax.ShapeDtypeStruct((NZ, *slab), bf16), jax.ShapeDtypeStruct((ROWS, COLS), bf16)),
        in_specs=[vmem] * 3,
        out_specs=[hbm] * 2,
        scratch_shapes=[pltpu.SemaphoreType.DMA((9,))],
        compiler_params=pltpu.CompilerParams(vmem_limit_bytes=32 * 2**20),
    )(full, own_params.reshape(slab), own_moment)
    return new_params.reshape(NZ * ROWS, COLS), new_momentum


def solution(mesh):
    return jax.shard_map(
        local, mesh=mesh, in_specs=(P("rep", "fsdp", None), P("rep", "fsdp", None), P("fsdp", None), P("fsdp", None)),
        out_specs=(P(), P("fsdp", None)), check_vma=False
    )
```

time: 167 us -> 64.7 us (0.39)
  waiting for transfers between devices: 93.1 us -> 0 us
  Pallas kernels: 0 us -> 59.4 us
  blocking collectives: 42.9 us -> 0 us
  between operations: 14.1 us -> 0.65 us
  local copies, waits for them, and re-layouts: 12.2 us -> 4.38 us
  other arithmetic: 4.57 us -> 0 us
    all_gather x1 -> x0, waiting for transfers between devices: 93.1 us -> none  [local(): new_params = lax.all_gather(updated, 'fsdp', axis=0, tiled=True)]
    pallas_call x0 -> x2, Pallas kernels: none -> 59.4 us  [the longest x1 55.7 us: local(): pl.pallas_call(exchange, name='exchange', out_shape=(pltpu.VMEM((NZ, *sla...]
    all_to_all x4 -> x0, blocking collectives: 42.9 us -> none  [the longest x2 20 us: sent_to_all(): return lax.all_to_all(copies, axis, split_axis=0, concat_axis=0, tiled=True)]
    unnamed x7 -> x8, local copies, waits for them, and re-layouts: 9.05 us -> 4.38 us
    mul x3 -> x0, local copies, waits for them, and re-layouts: 2.93 us -> none  [dequantize(): code_rows.astype(jnp.float32).reshape(count, width // 128, 128)]
    convert_element_type x1 -> x0, other arithmetic: 2.05 us -> none  [outer_update(): return (updated, moment.astype(jnp.bfloat16))]
    transpose x1 -> x0, other arithmetic: 1.94 us -> none  [in_blocks(): return jnp.moveaxis(shard.reshape(*before, peers, -1, *after), dim, 0)]
  transfers between devices with their start and end apart: 1 -> 0, of which waited for: 1 -> 0; matrix products, arithmetic and copies ran while one was open for 0% -> 0% of each run, Pallas kernels for 0% -> 0%
where the time goes in v1:
time: 64.7 us; the launch traced here: 64.4 us
  Pallas kernels  59.4 us (92%)
  local copies, waits for them, and re-layouts  4.38 us (7%)
  between operations  0.65 us (1%)
    pallas_call x1, Pallas kernels, local(): pl.pallas_call(exchange, name='exchange', out_shape=(pltpu.VMEM((NZ, *sla...  55.7 us
    unnamed x8, local copies, waits for them, and re-layouts  4.38 us
    pallas_call x1, Pallas kernels, local(): pl.pallas_call(write_out, name='write_out', out_shape=(jax.ShapeDtypeStru...  3.7 us

profile of v1, /device:TPU:1, one launch (start us, length us, event | category | flops | bytes accessed | tf_op | source)
XLA Modules:
  0.0 64.4 jit_solution(12874964611817455874)
XLA Ops:
  0.6 0.0 copy-start
  0.6 1.2 %copy-done = bf16[1,512,1024]{2,1,0:T(8,128)(2,1)S(1)} copy-done((bf16[1,512,1024]{2,1,0:T(8,128)(2,1)S(1)}, bf16[1,512,1024]{2,1,0:T(8,128)(2,1)}, u32[]{:S(2)}) %copy-start) | copy-done | bytes 1048600
  1.9 0.0 copy-start.1
  1.9 1.2 %copy-done.1 = bf16[512,1024]{1,0:T(8,128)(2,1)S(1)} copy-done((bf16[512,1024]{1,0:T(8,128)(2,1)S(1)}, bf16[512,1024]{1,0:T(8,128)(2,1)}, u32[]{:S(2)}) %copy-start.1) | copy-done | bytes 1048600
  3.1 0.0 copy-start.2
  3.1 1.2 %copy-done.2 = bf16[512,1024]{1,0:T(8,128)(2,1)S(1)} copy-done((bf16[512,1024]{1,0:T(8,128)(2,1)S(1)}, bf16[512,1024]{1,0:T(8,128)(2,1)}, u32[]{:S(2)}) %copy-start.2) | copy-done | bytes 1048600
  4.3 0.0 copy-start.3
  4.3 0.7 %copy-done.3 = f32[1,512,8]{1,2,0:T(8,128)S(1)} copy-done((f32[1,512,8]{1,2,0:T(8,128)S(1)}, f32[1,512,8]{1,2,0:T(8,128)}, u32[]{:S(2)}) %copy-start.3) | copy-done | bytes 16408
  5.0 55.7 %exchange.1 = (bf16[8,2,4,4,16,1024]{5,4,3,2,1,0:T(8,128)(2,1)S(1)}, bf16[512,1024]{1,0:T(8,128)(2,1)S(1)}, bf16[512,1024]{1,0:T(8,128)(2,1)S(1)}) custom-call(bf16[512,1024]{1,0:T(8,128)(2,1)S(1)} %bitcast.6, f32[8,512]{1,0:T(8,128)S(1)} %bitcast.8, bf16[512,1024]{1,0:T(8,128)(2,1)S(1)} %copy-done.1, bf16[512,1024]{1,0:T(8,128)(2,1)S(1)} %copy-done.2), custom_call_target="tpu_custom_call" | custom-call | tf_op jit(solution)/shard_map/exchange/pallas_call | solution.py:256
  60.7 3.7 %write_out.1 = (bf16[8,2,4,4,16,1024]{5,4,3,2,1,0:T(8,128)(2,1)}, bf16[512,1024]{1,0:T(8,128)(2,1)}) custom-call(bf16[8,2,4,4,16,1024]{5,4,3,2,1,0:T(8,128)(2,1)S(1)} %get-tuple-element.7.full, bf16[2,4,4,16,1024]{4,3,2,1,0:T(8,128)(2,1)S(1)} %bitcast.7, bf16[512,1024]{1,0:T(8,128)(2,1)S(1)} %get-tuple-element.9.own_moment), custom_call_target="tpu_custom_call" | custom-call | tf_op jit(solution)/shard_map/write_out/pallas_call | solution.py:281
Async XLA Ops:
  0.6 1.2 %copy-start = (bf16[1,512,1024]{2,1,0:T(8,128)(2,1)S(1)}, bf16[1,512,1024]{2,1,0:T(8,128)(2,1)}, u32[]{:S(2)}) copy-start(bf16[1,512,1024]{2,1,0:T(8,128)(2,1)} %param.4) | copy-start | bytes 3145732
  1.9 1.2 %copy-start.1 = (bf16[512,1024]{1,0:T(8,128)(2,1)S(1)}, bf16[512,1024]{1,0:T(8,128)(2,1)}, u32[]{:S(2)}) copy-start(bf16[512,1024]{1,0:T(8,128)(2,1)} %params.1) | copy-start | bytes 3145732
  3.1 1.2 %copy-start.2 = (bf16[512,1024]{1,0:T(8,128)(2,1)S(1)}, bf16[512,1024]{1,0:T(8,128)(2,1)}, u32[]{:S(2)}) copy-start(bf16[512,1024]{1,0:T(8,128)(2,1)} %momentum.1) | copy-start | bytes 3145732
  4.3 0.7 %copy-start.3 = (f32[1,512,8]{1,2,0:T(8,128)S(1)}, f32[1,512,8]{1,2,0:T(8,128)}, u32[]{:S(2)}) copy-start(f32[1,512,8]{1,2,0:T(8,128)} %param.5) | copy-start | bytes 49156

commit v2 on v1

v2 whole, which is shorter than its diff:
```python
import functools

import jax
import jax.numpy as jnp
from jax import lax
from jax.experimental import pallas as pl
from jax.experimental.pallas import tpu as pltpu
from jax.sharding import PartitionSpec as P

MESH = pl.DeviceIdType.MESH
NX, NY, NZ = 4, 4, 8
ROWS, COLS, BLOCK = 512, 1024, 128
HALF = ROWS // 2
PIECE = 16
NEAR = (0, 1, -1, 2, -2, 3, -3, 4)
PLACE = {d: i for i, d in enumerate(NEAR)} | {-4: 7}
AB = 640
C = (AB, COLS - AB)
WAVES = ((0, 1, 384), (1, 2, 256), (3, 2, 256), (5, 3, 384))
SPLIT = {C: ((640, 128), (768, 256)), (0, AB): ((0, 384), (384, 256))}
LINE = (1, -1, 2)
PLANE = [(dx, dy) for dy in (0, 1, -1, 2) for dx in (0, 1, -1, 2) if (dx, dy) != (0, 0)]
GROUPS = ("A", "B")
COPIES = 160
ORDER = (
    ("line_c",), ("line_ab",), ("sum_c",), ("sum_ab",), ("second", 1), ("ring_start",), ("third", 0), ("second", 2), ("second", 3),
    ("third", 1), ("onward", 0), ("ring", 1), ("third", 2), ("onward", 1), ("third", 3), ("finish", 0),
    ("ring", 2), ("onward", 2), ("finish", 1), ("own",), ("onward", 3), ("finish", 2), ("ring", 3), ("finish", 3), ("ring", 4),
)


def position():
    r, z = lax.axis_index("rep"), lax.axis_index("fsdp")
    return lax.rem(lax.div(r, 2), NX), lax.div(r, 2 * NX), z, lax.rem(r, 2)


def step_of(delta, params, momentum):
    delta = delta.astype(jnp.float32)
    moment = 0.9 * momentum.astype(jnp.float32) + delta
    updated = params.astype(jnp.float32) - 0.7 * (delta + 0.9 * moment)
    return updated.astype(jnp.bfloat16), moment.astype(jnp.bfloat16)


def exchange(codes, scales, params, momentum, full, own_params, own_moment,
             codes_v, scales_v, params_v, momentum_v, sib_out, sib_in, chip_sum, line_in, line_sum, last_in, piece, ring,
             load_sem, send_sem, recv_sem):
    x, y, z, c = position()
    other = 1 - c

    known = {}

    def device(dx=0, dy=0, dz=0, dc=0):
        to = (dx % NX, dy % NY, dz % NZ, dc)
        if to not in known:
            across = lax.rem(x + to[0], NX) if to[0] else x
            along_y = lax.rem(y + to[1], NY) if to[1] else y
            known[to] = (along_y * NX + across) * 2 + (other if dc else c), lax.rem(z + to[2], NZ) if to[2] else z
        return known[to]

    loads = [pltpu.make_async_copy(src, dst, load_sem.at[i]) for i, (src, dst) in enumerate(
        ((codes, codes_v), (scales, scales_v), (params, params_v), (momentum, momentum_v)))]
    for load in loads:
        load.start()

    barrier = pltpu.get_barrier_semaphore()
    partners = [dict(dc=1)] + [dict(dx=dx, dy=dy) for dx, dy in PLANE] + [dict(dz=dz) for dz in NEAR[1:]]
    for partner in partners:
        pl.semaphore_signal(barrier, inc=1, device_id=device(**partner), device_id_type=MESH)

    sent = []

    def together(ref):
        sent.append(ref)
        return len(sent) - 1

    def send(src, dst, group=None, **to):
        i = together(dst) if group is None else group
        pltpu.make_async_remote_copy(src, dst, send_sem.at[i], recv_sem.at[i],
                                     device_id=device(**to), device_id_type=MESH).start()
        return i

    def got(*groups):
        for i in groups:
            pltpu.make_async_copy(sent[i], sent[i], recv_sem.at[i]).wait()

    def left(*groups):
        for i in groups:
            pltpu.make_async_copy(sent[i], sent[i], send_sem.at[i]).wait()

    def dequantized(half, chunk, group):
        start = pl.multiple_of(half * HALF + chunk * 128, 128)
        turned = scales_v[:, pl.ds(start, 128)].T
        for block in range(group[0] // BLOCK, (group[0] + group[1]) // BLOCK):
            cols = slice(block * BLOCK, (block + 1) * BLOCK)
            yield cols, codes_v[pl.ds(start, 128), cols].astype(jnp.float32) * turned[:, block:block + 1]

    groups = (C, (0, AB))
    loads[0].wait()
    loads[1].wait()
    halves = []
    for group in groups:
        for chunk in range(2):
            rows = slice(chunk * 128, (chunk + 1) * 128)
            for cols, terms in dequantized(other, chunk, group):
                sib_out[rows, cols] = terms.astype(jnp.bfloat16)
        if group is C:
            pl.semaphore_wait(barrier, len(partners))
        cols = pl.ds(*group)
        halves.append(send(sib_out.at[:, cols], sib_in.at[:, cols], dc=1))

    first_step, second_step = {}, {}
    for group, half in zip(groups, halves):
        got(half)
        for chunk in range(2):
            rows = slice(chunk * 128, (chunk + 1) * 128)
            for cols, terms in dequantized(c, chunk, group):
                total = terms + sib_in[rows, cols].astype(jnp.float32)
                chip_sum[2 * chunk:2 * chunk + 2, :, :, cols] = total.astype(jnp.bfloat16).reshape(2, NX, PIECE, BLOCK)
        first_step[group] = together(line_in.at[:, :, :, pl.ds(*group)])
        along_x, along_y = (pl.ds(*cols) for cols in SPLIT[group])
        for i, d in enumerate(LINE):
            send(chip_sum.at[:, lax.rem(x + d + NX, NX), :, along_x], line_in.at[i, :, :, along_x], first_step[group], dx=d)
            send(chip_sum.at[lax.rem(y + d + NY, NY), :, :, along_y], line_in.at[i, :, :, along_y], first_step[group], dy=d)

    start = pl.multiple_of(c * HALF + y * 64 + x * PIECE, PIECE)

    def sum_line(group):
        got(first_step[group])
        for (low, width), own in zip(SPLIT[group], (chip_sum.at[:, x], chip_sum.at[y])):
            cols = slice(low, low + width)
            total = own[:, :, cols].astype(jnp.float32)
            for i in range(len(LINE)):
                total = total + line_in[i, :, :, cols].astype(jnp.float32)
            line_sum[:, :, cols] = total.astype(jnp.bfloat16)
        second_step[group] = together(last_in.at[:, :, pl.ds(*group)])
        along_x, along_y = (pl.ds(*cols) for cols in SPLIT[group])
        for i, d in enumerate(LINE):
            send(line_sum.at[lax.rem(y + d + NY, NY), :, along_x], last_in.at[i, :, along_x], second_step[group], dy=d)
            send(line_sum.at[lax.rem(x + d + NX, NX), :, along_y], last_in.at[i, :, along_y], second_step[group], dx=d)

    def summed(group):
        got(second_step[group])
        for (low, width), own in zip(SPLIT[group], (y, x)):
            cols = slice(low, low + width)
            total = line_sum[own, :, cols].astype(jnp.float32)
            for i in range(len(LINE)):
                total = total + last_in[i, :, cols].astype(jnp.float32)
            full[0, c, y, x, :, cols] = (total / 32).astype(jnp.bfloat16)
        return full[0, c, y, x, :, group[0]:group[0] + group[1]]

    def columns(wave, group):
        width = WAVES[wave][2]
        return pl.ds(0, width) if group == "A" else pl.ds(width, AB - width)

    def at(wave, rows_y, rows_x, group):
        first, count, _ = WAVES[wave]
        return full.at[pl.ds(first, count), c, rows_y, rows_x, :, columns(wave, group)]

    def second(wave, group):
        block = at(wave, y, x, group)
        three = together(at(wave, y, pl.ds(0, 3), group))
        for d in (1, -1, 2):
            send(block, block, three, **{"dx" if group == "A" else "dy": d})
        return three

    def brought(wave, group, back, rows=pl.ds(0, 4)):
        if group == "A":
            return at(wave, lax.rem(y - back + NY, NY), rows, group)
        return at(wave, rows, lax.rem(x - back + NX, NX), group)

    def third(wave, group):
        axis = "dy" if group == "A" else "dx"
        own = brought(wave, group, 0)
        return send(own, own, **{axis: 1}), send(own, own, **{axis: -1})

    def onward(wave, group, copies):
        axis = "dy" if group == "A" else "dx"
        going = []
        for i, (copy, step) in enumerate(zip(copies, (1, -1))):
            half = brought(wave, group, step, pl.ds(2 * i, 2))
            got(copy)
            going.append(send(half, half, **{axis: step}))
        return going

    def to_sibling(block):
        return send(block, block, dc=1)

    S2, S3, S4, handed = {}, {}, {}, []

    along = {}
    plane_c = together(sib_in.at[pl.ds(0, len(PLANE) * PIECE), pl.ds(*C)])

    def sum_c():
        summed(C)
        block = full.at[0, c, y, x, :, pl.ds(*C)]
        for dx, dy in PLANE:
            send(block, block, plane_c, dx=dx, dy=dy)

    def sum_ab():
        loads[2].wait()
        loads[3].wait()
        delta = summed(groups[1])
        piece[...] = step_of(delta, params_v[pl.ds(start, PIECE), :AB], momentum_v[pl.ds(start, PIECE), :AB])[0]
        for first, count, _ in WAVES[1:]:
            along[first] = together(full.at[pl.ds(first, count), c, y, x, :, pl.ds(0, AB)])
            for place in range(first, first + count):
                send(piece, full.at[place, c, y, x, :, pl.ds(0, AB)], along[first], dz=-NEAR[place])
        for group in GROUPS:
            S2[0, group] = second(0, group)

    def start_second(wave):
        got(along[WAVES[wave][0]])
        for group in GROUPS:
            S2[wave, group] = second(wave, group)

    def start_third(wave):
        for group in GROUPS:
            got(S2[wave, group])
            S3[wave, group] = third(wave, group)

    def start_onward(wave):
        for group in GROUPS:
            S4[wave, group] = onward(wave, group, S3[wave, group])

    own_parts = []

    def finish(wave):
        for group in GROUPS:
            got(*S4[wave, group])
            (handed if wave else own_parts).append(to_sibling(at(wave, slice(None), slice(None), group)))

    def ring_at(d, part):
        return full.at[PLACE[d], c, pl.ds(2 * part, 2), :, :, pl.ds(*C)]

    up, down = {}, {}

    def ring_start():
        got(plane_c)
        for row in range(NY):
            first = pl.multiple_of(c * HALF + row * 64, 64)
            cols = slice(C[0], C[0] + C[1])
            moved = full[0, c, row, :, :, cols].reshape(64, C[1])
            ring[row] = step_of(moved, params_v[pl.ds(first, 64), cols], momentum_v[pl.ds(first, 64), cols])[0].reshape(
                NX, PIECE, C[1])
            if row % 2:
                part = row // 2
                own = ring.at[pl.ds(2 * part, 2)]
                up[1, part] = send(own, ring_at(-1, part), dz=1)
                down[1, part] = send(own, ring_at(1, part), dz=-1)
        own_parts.append(to_sibling(full.at[0, c, :, :, :, pl.ds(*C)]))

    def ring_step(n):
        for part in range(2):
            if n < 4 or part == 0:
                got(up[n, part])
            if n < 4 or part == 1:
                got(down[n, part])
            if n < 3 or (n == 3 and part == 0):
                up[n + 1, part] = send(ring_at(-n, part), ring_at(-n - 1, part), dz=1)
            if n < 3 or (n == 3 and part == 1):
                down[n + 1, part] = send(ring_at(n, part), ring_at(n + 1, part), dz=-1)
        handed.append(to_sibling(full.at[pl.ds(PLACE[n], 2 if n < 4 else 1), c, :, :, :, pl.ds(*C)]))

    def own_rows():
        got(*own_parts)
        for i in range(2):
            for row in range(NY):
                first = i * HALF + row * 64
                moved = full[0, i, row].reshape(64, COLS)
                updated, moment = step_of(moved, params_v[first:first + 64], momentum_v[first:first + 64])
                own_params[first:first + 64] = updated
                own_moment[first:first + 64] = moment

    for act, *which in ORDER:
        {"line_c": lambda: sum_line(C), "line_ab": lambda: sum_line(groups[1]), "sum_c": sum_c, "sum_ab": sum_ab, "second": start_second, "third": start_third, "onward": start_onward,
         "finish": finish, "ring": ring_step, "ring_start": ring_start, "own": own_rows}[act](*which)
    left(*(i for i in range(len(sent)) if i not in handed))
    got(*handed)
    left(*handed)


def write_out(full, own_params, own_moment, new_params, new_momentum, sem):
    z = lax.axis_index("fsdp")
    copies = []
    for i, d in enumerate(NEAR[1:], 1):
        copies.append(pltpu.make_async_copy(full.at[i], new_params.at[lax.rem(z + d + NZ, NZ)], sem.at[i]))
    copies.append(pltpu.make_async_copy(own_params, new_params.at[z], sem.at[0]))
    copies.append(pltpu.make_async_copy(own_moment, new_momentum, sem.at[8]))
    for copy in copies:
        copy.start()
    for copy in copies:
        copy.wait()


def local(codes, block_scales, params, momentum):
    bf16 = jnp.bfloat16
    slab = (2, NY, NX, PIECE, COLS)
    hbm, vmem = pl.BlockSpec(memory_space=pltpu.HBM), pl.BlockSpec(memory_space=pltpu.VMEM)
    full, own_params, own_moment = pl.pallas_call(
        exchange,
        name="exchange",
        out_shape=(pltpu.VMEM((NZ, *slab), bf16), pltpu.VMEM((ROWS, COLS), bf16), pltpu.VMEM((ROWS, COLS), bf16)),
        in_specs=[hbm] * 4,
        out_specs=[vmem] * 3,
        scratch_shapes=[
            pltpu.VMEM((ROWS, COLS), bf16),
            pltpu.VMEM((COLS // BLOCK, ROWS), jnp.float32),
            pltpu.VMEM((ROWS, COLS), bf16),
            pltpu.VMEM((ROWS, COLS), bf16),
            pltpu.VMEM((HALF, COLS), bf16),
            pltpu.VMEM((HALF, COLS), bf16),
            pltpu.VMEM((NY, NX, PIECE, COLS), bf16),
            pltpu.VMEM((len(LINE), NY, PIECE, COLS), bf16),
            pltpu.VMEM((NY, PIECE, COLS), bf16),
            pltpu.VMEM((len(LINE), PIECE, COLS), bf16),
            pltpu.VMEM((PIECE, AB), bf16),
            pltpu.VMEM((NY, NX, PIECE, C[1]), bf16),
            pltpu.SemaphoreType.DMA((4,)),
            pltpu.SemaphoreType.DMA((COPIES,)),
            pltpu.SemaphoreType.DMA((COPIES,)),
        ],
        compiler_params=pltpu.CompilerParams(
            collective_id=0, has_side_effects=True, vmem_limit_bytes=50 * 2**20
        ),
    )(codes[0], block_scales[0].T, params, momentum)
    new_params, new_momentum = pl.pallas_call(
        write_out,
        name="write_out",
        out_shape=(jax.ShapeDtypeStruct((NZ, *slab), bf16), jax.ShapeDtypeStruct((ROWS, COLS), bf16)),
        in_specs=[vmem] * 3,
        out_specs=[hbm] * 2,
        scratch_shapes=[pltpu.SemaphoreType.DMA((9,))],
        compiler_params=pltpu.CompilerParams(vmem_limit_bytes=32 * 2**20),
    )(full, own_params.reshape(slab), own_moment)
    return new_params.reshape(NZ * ROWS, COLS), new_momentum


def solution(mesh):
    return jax.shard_map(
        local, mesh=mesh, in_specs=(P("rep", "fsdp", None), P("rep", "fsdp", None), P("fsdp", None), P("fsdp", None)),
        out_specs=(P(), P("fsdp", None)), check_vma=False
    )
```

time: 64.7 us -> 54.5 us (0.84)
  Pallas kernels: 59.4 us -> 53.8 us
  local copies, waits for them, and re-layouts: 4.38 us -> 0 us
    pallas_call x1, Pallas kernels: 55.7 us -> 50.1 us  [local(): pl.pallas_call(exchange, name='exchange', out_shape=(pltpu.VMEM((NZ, *sla...]
    unnamed x8 -> x0, local copies, waits for them, and re-layouts: 4.38 us -> none
where the time goes in v2:
time: 54.5 us
  Pallas kernels  53.8 us (99%)
  between operations  0.64 us (1%)
    pallas_call x1, Pallas kernels, local(): pl.pallas_call(exchange, name='exchange', out_shape=(pltpu.VMEM((NZ, *sla...  50.1 us
    pallas_call x1, Pallas kernels, local(): pl.pallas_call(write_out, name='write_out', out_shape=(jax.ShapeDtypeStru...  3.7 us

profile of v2, /device:TPU:1, one launch (start us, length us, event | category | flops | bytes accessed | tf_op | source)
XLA Modules:
  0.0 54.5 jit_solution(18063212723748102608)
XLA Ops:
  0.6 50.1 %exchange.1 = (bf16[8,2,4,4,16,1024]{5,4,3,2,1,0:T(8,128)(2,1)S(1)}, bf16[512,1024]{1,0:T(8,128)(2,1)S(1)}, bf16[512,1024]{1,0:T(8,128)(2,1)S(1)}) custom-call(bf16[512,1024]{1,0:T(8,128)(2,1)} %bitcast.7, f32[8,512]{1,0:T(8,128)} %bitcast.8, bf16[512,1024]{1,0:T(8,128)(2,1)} %params.1, bf16[512,1024]{1,0:T(8,128)(2,1)} %momentum.1), custom_call_target="tpu_custom_call" | custom-call | tf_op jit(solution)/shard_map/exchange/pallas_call | solution.py:299
  50.8 3.7 %write_out.1 = (bf16[8,2,4,4,16,1024]{5,4,3,2,1,0:T(8,128)(2,1)}, bf16[512,1024]{1,0:T(8,128)(2,1)}) custom-call(bf16[8,2,4,4,16,1024]{5,4,3,2,1,0:T(8,128)(2,1)S(1)} %get-tuple-element.7.full, bf16[2,4,4,16,1024]{4,3,2,1,0:T(8,128)(2,1)S(1)} %bitcast.6, bf16[512,1024]{1,0:T(8,128)(2,1)S(1)} %get-tuple-element.9.own_moment), custom_call_target="tpu_custom_call" | custom-call | tf_op jit(solution)/shard_map/write_out/pallas_call | solution.py:326

commit v3 on v2

--- a/solution.py
+++ b/solution.py
@@ -22,11 +22,7 @@
 PLANE = [(dx, dy) for dy in (0, 1, -1, 2) for dx in (0, 1, -1, 2) if (dx, dy) != (0, 0)]
 GROUPS = ("A", "B")
 COPIES = 160
-ORDER = (
-    ("line_c",), ("line_ab",), ("sum_c",), ("sum_ab",), ("second", 1), ("ring_start",), ("third", 0), ("second", 2), ("second", 3),
-    ("third", 1), ("onward", 0), ("ring", 1), ("third", 2), ("onward", 1), ("third", 3), ("finish", 0),
-    ("ring", 2), ("onward", 2), ("finish", 1), ("own",), ("onward", 3), ("finish", 2), ("ring", 3), ("finish", 3), ("ring", 4),
-)
+ORDER = (("line_c",), ("line_ab",), ("sum_c",), ("sum_ab",), ("second", 1), ("ring_start",), ("second", 2), ("third", 0), ("second", 3), ("third", 1), ("ring", 1), ("third", 2), ("onward", 0), ("third", 3), ("onward", 1), ("ring", 2), ("finish", 0), ("onward", 2), ("onward", 3), ("finish", 1), ("ring", 3), ("finish", 2), ("finish", 3), ("own",), ("ring", 4))
 
 
 def position():
@@ -59,7 +55,7 @@
 
     loads = [pltpu.make_async_copy(src, dst, load_sem.at[i]) for i, (src, dst) in enumerate(
         ((codes, codes_v), (scales, scales_v), (params, params_v), (momentum, momentum_v)))]
-    for load in loads:
+    for load in loads[:2]:
         load.start()
 
     barrier = pltpu.get_barrier_semaphore()
@@ -97,12 +93,16 @@
     groups = (C, (0, AB))
     loads[0].wait()
     loads[1].wait()
+    for load in loads[2:]:
+        load.start()
     halves = []
     for group in groups:
-        for chunk in range(2):
-            rows = slice(chunk * 128, (chunk + 1) * 128)
+        @pl.loop(0, 2)
+        def _(chunk):
+            rows = pl.ds(pl.multiple_of(chunk * 128, 128), 128)
             for cols, terms in dequantized(other, chunk, group):
                 sib_out[rows, cols] = terms.astype(jnp.bfloat16)
+
         if group is C:
             pl.semaphore_wait(barrier, len(partners))
         cols = pl.ds(*group)
@@ -111,11 +111,14 @@
     first_step, second_step = {}, {}
     for group, half in zip(groups, halves):
         got(half)
-        for chunk in range(2):
-            rows = slice(chunk * 128, (chunk + 1) * 128)
+
+        @pl.loop(0, 2)
+        def _(chunk):
+            rows = pl.ds(pl.multiple_of(chunk * 128, 128), 128)
             for cols, terms in dequantized(c, chunk, group):
                 total = terms + sib_in[rows, cols].astype(jnp.float32)
-                chip_sum[2 * chunk:2 * chunk + 2, :, :, cols] = total.astype(jnp.bfloat16).reshape(2, NX, PIECE, BLOCK)
+                chip_sum[pl.ds(2 * chunk, 2), :, :, cols] = total.astype(jnp.bfloat16).reshape(2, NX, PIECE, BLOCK)
+
         first_step[group] = together(line_in.at[:, :, :, pl.ds(*group)])
         along_x, along_y = (pl.ds(*cols) for cols in SPLIT[group])
         for i, d in enumerate(LINE):
@@ -230,46 +233,45 @@
             (handed if wave else own_parts).append(to_sibling(at(wave, slice(None), slice(None), group)))
 
     def ring_at(d, part):
-        return full.at[PLACE[d], c, pl.ds(2 * part, 2), :, :, pl.ds(*C)]
+        return full.at[PLACE[d], c, part, :, :, pl.ds(*C)]
 
     up, down = {}, {}
 
     def ring_start():
         got(plane_c)
-        for row in range(NY):
+        cols = slice(C[0], C[0] + C[1])
+
+        @pl.loop(0, NY)
+        def _(row):
             first = pl.multiple_of(c * HALF + row * 64, 64)
-            cols = slice(C[0], C[0] + C[1])
             moved = full[0, c, row, :, :, cols].reshape(64, C[1])
             ring[row] = step_of(moved, params_v[pl.ds(first, 64), cols], momentum_v[pl.ds(first, 64), cols])[0].reshape(
                 NX, PIECE, C[1])
-            if row % 2:
-                part = row // 2
-                own = ring.at[pl.ds(2 * part, 2)]
-                up[1, part] = send(own, ring_at(-1, part), dz=1)
-                down[1, part] = send(own, ring_at(1, part), dz=-1)
+
+        for part in range(NY):
+            up[1, part] = send(ring.at[part], ring_at(-1, part), dz=1)
+            down[1, part] = send(ring.at[part], ring_at(1, part), dz=-1)
         own_parts.append(to_sibling(full.at[0, c, :, :, :, pl.ds(*C)]))
 
     def ring_step(n):
-        for part in range(2):
-            if n < 4 or part == 0:
+        for part in range(NY):
+            if n < 4 or part < 2:
                 got(up[n, part])
-            if n < 4 or part == 1:
+            if n < 4 or part >= 2:
                 got(down[n, part])
-            if n < 3 or (n == 3 and part == 0):
+            if n < 3 or (n == 3 and part < 2):
                 up[n + 1, part] = send(ring_at(-n, part), ring_at(-n - 1, part), dz=1)
-            if n < 3 or (n == 3 and part == 1):
+            if n < 3 or (n == 3 and part >= 2):
                 down[n + 1, part] = send(ring_at(n, part), ring_at(n + 1, part), dz=-1)
         handed.append(to_sibling(full.at[pl.ds(PLACE[n], 2 if n < 4 else 1), c, :, :, :, pl.ds(*C)]))
 
     def own_rows():
         got(*own_parts)
-        for i in range(2):
-            for row in range(NY):
-                first = i * HALF + row * 64
-                moved = full[0, i, row].reshape(64, COLS)
-                updated, moment = step_of(moved, params_v[first:first + 64], momentum_v[first:first + 64])
-                own_params[first:first + 64] = updated
-                own_moment[first:first + 64] = moment
+        @pl.loop(0, 2 * NY)
+        def _(row):
+            rows = pl.ds(pl.multiple_of(row * 64, 64), 64)
+            moved = full[0, lax.div(row, NY), lax.rem(row, NY)].reshape(64, COLS)
+            own_params[rows], own_moment[rows] = step_of(moved, params_v[rows], momentum_v[rows])
 
     for act, *which in ORDER:
         {"line_c": lambda: sum_line(C), "line_ab": lambda: sum_line(groups[1]), "sum_c": sum_c, "sum_ab": sum_ab, "second": start_second, "third": start_third, "onward": start_onward,

time: 54.5 us -> 53.3 us (0.978)
  Pallas kernels: 53.8 us -> 52.5 us
    pallas_call x1, Pallas kernels: 50.1 us -> 48.8 us  [local(): pl.pallas_call(exchange, name='exchange', out_shape=(pltpu.VMEM((NZ, *sla...]
where the time goes in v3:
time: 53.3 us; the launch traced here: 53.2 us
  Pallas kernels  52.5 us (98%)
  between operations  0.64 us (1%)
    pallas_call x1, Pallas kernels, local(): pl.pallas_call(exchange, name='exchange', out_shape=(pltpu.VMEM((NZ, *sla...  48.8 us
    pallas_call x1, Pallas kernels, local(): pl.pallas_call(write_out, name='write_out', out_shape=(jax.ShapeDtypeStru...  3.7 us

profile of v3, /device:TPU:1, one launch (start us, length us, event | category | flops | bytes accessed | tf_op | source)
XLA Modules:
  0.0 53.2 jit_solution(12775573482981777932)
XLA Ops:
  0.6 48.8 %exchange.1 = (bf16[8,2,4,4,16,1024]{5,4,3,2,1,0:T(8,128)(2,1)S(1)}, bf16[512,1024]{1,0:T(8,128)(2,1)S(1)}, bf16[512,1024]{1,0:T(8,128)(2,1)S(1)}) custom-call(bf16[512,1024]{1,0:T(8,128)(2,1)} %bitcast.7, f32[8,512]{1,0:T(8,128)} %bitcast.8, bf16[512,1024]{1,0:T(8,128)(2,1)} %params.1, bf16[512,1024]{1,0:T(8,128)(2,1)} %momentum.1), custom_call_target="tpu_custom_call" | custom-call | tf_op jit(solution)/shard_map/exchange/pallas_call | solution.py:301
  49.5 3.7 %write_out.1 = (bf16[8,2,4,4,16,1024]{5,4,3,2,1,0:T(8,128)(2,1)}, bf16[512,1024]{1,0:T(8,128)(2,1)}) custom-call(bf16[8,2,4,4,16,1024]{5,4,3,2,1,0:T(8,128)(2,1)S(1)} %get-tuple-element.7.full, bf16[2,4,4,16,1024]{4,3,2,1,0:T(8,128)(2,1)S(1)} %bitcast.6, bf16[512,1024]{1,0:T(8,128)(2,1)S(1)} %get-tuple-element.9.own_moment), custom_call_target="tpu_custom_call" | custom-call | tf_op jit(solution)/shard_map/write_out/pallas_call | solution.py:328

commit v4 on v3

--- a/solution.py
+++ b/solution.py
@@ -22,7 +22,7 @@
 PLANE = [(dx, dy) for dy in (0, 1, -1, 2) for dx in (0, 1, -1, 2) if (dx, dy) != (0, 0)]
 GROUPS = ("A", "B")
 COPIES = 160
-ORDER = (("line_c",), ("line_ab",), ("sum_c",), ("sum_ab",), ("second", 1), ("ring_start",), ("second", 2), ("third", 0), ("second", 3), ("third", 1), ("ring", 1), ("third", 2), ("onward", 0), ("third", 3), ("onward", 1), ("ring", 2), ("finish", 0), ("onward", 2), ("onward", 3), ("finish", 1), ("ring", 3), ("finish", 2), ("finish", 3), ("own",), ("ring", 4))
+ORDER = (("line_c",), ("line_ab",), ("sum_c",), ("sum_ab",), ("second", 1), ("ring_start",), ("second", 2), ("third", 0), ("second", 3), ("third", 1), ("ring", 1, 0, 2), ("third", 2), ("ring", 1, 2, 4), ("onward", 0), ("third", 3), ("onward", 1), ("ring", 2, 0, 2), ("finish", 0), ("onward", 2), ("ring", 2, 2, 4), ("onward", 3), ("finish", 1), ("ring", 3, 0, 2), ("finish", 2), ("ring", 3, 2, 4), ("finish", 3), ("own",), ("ring", 4))
 
 
 def position():
@@ -253,8 +253,8 @@
             down[1, part] = send(ring.at[part], ring_at(1, part), dz=-1)
         own_parts.append(to_sibling(full.at[0, c, :, :, :, pl.ds(*C)]))
 
-    def ring_step(n):
-        for part in range(NY):
+    def ring_step(n, low=0, high=NY):
+        for part in range(low, high):
             if n < 4 or part < 2:
                 got(up[n, part])
             if n < 4 or part >= 2:
@@ -263,7 +263,8 @@
                 up[n + 1, part] = send(ring_at(-n, part), ring_at(-n - 1, part), dz=1)
             if n < 3 or (n == 3 and part >= 2):
                 down[n + 1, part] = send(ring_at(n, part), ring_at(n + 1, part), dz=-1)
-        handed.append(to_sibling(full.at[pl.ds(PLACE[n], 2 if n < 4 else 1), c, :, :, :, pl.ds(*C)]))
+        if high == NY:
+            handed.append(to_sibling(full.at[pl.ds(PLACE[n], 2 if n < 4 else 1), c, :, :, :, pl.ds(*C)]))
 
     def own_rows():
         got(*own_parts)

time: 53.3 us -> 53.1 us (level)
  no operation moved by 1% of the time
where the time goes in v4:
time: 53.1 us; the launch traced here: 53 us
  Pallas kernels  52.4 us (99%)
  between operations  0.64 us (1%)
    pallas_call x1, Pallas kernels, local(): pl.pallas_call(exchange, name='exchange', out_shape=(pltpu.VMEM((NZ, *sla...  48.7 us
    pallas_call x1, Pallas kernels, local(): pl.pallas_call(write_out, name='write_out', out_shape=(jax.ShapeDtypeStru...  3.7 us

profile of v4, /device:TPU:1, one launch (start us, length us, event | category | flops | bytes accessed | tf_op | source)
XLA Modules:
  0.0 53.0 jit_solution(932680060437922836)
XLA Ops:
  0.6 48.7 %exchange.1 = (bf16[8,2,4,4,16,1024]{5,4,3,2,1,0:T(8,128)(2,1)S(1)}, bf16[512,1024]{1,0:T(8,128)(2,1)S(1)}, bf16[512,1024]{1,0:T(8,128)(2,1)S(1)}) custom-call(bf16[512,1024]{1,0:T(8,128)(2,1)} %bitcast.7, f32[8,512]{1,0:T(8,128)} %bitcast.8, bf16[512,1024]{1,0:T(8,128)(2,1)} %params.1, bf16[512,1024]{1,0:T(8,128)(2,1)} %momentum.1), custom_call_target="tpu_custom_call" | custom-call | tf_op jit(solution)/shard_map/exchange/pallas_call | solution.py:302
  49.3 3.7 %write_out.1 = (bf16[8,2,4,4,16,1024]{5,4,3,2,1,0:T(8,128)(2,1)}, bf16[512,1024]{1,0:T(8,128)(2,1)}) custom-call(bf16[8,2,4,4,16,1024]{5,4,3,2,1,0:T(8,128)(2,1)S(1)} %get-tuple-element.7.full, bf16[2,4,4,16,1024]{4,3,2,1,0:T(8,128)(2,1)S(1)} %bitcast.6, bf16[512,1024]{1,0:T(8,128)(2,1)S(1)} %get-tuple-element.9.own_moment), custom_call_target="tpu_custom_call" | custom-call | tf_op jit(solution)/shard_map/write_out/pallas_call | solution.py:329
